TPU v7x, 32 devices: a whole 2x2x4 slice. The times are simulated.
32 devices in a mesh: dp: 8 (over y, x, core), tensor: 4 (over z).
Axes of the slice: x: 2, y: 2, z: 4, core: 2. Of those that a mesh axis runs over, the one named last changes fastest.
Arguments:
- hidden: bfloat16 [1024, 8192], P('dp', 'tensor')
- rotation: float32 [8192, 8192], P('dp', 'tensor'), may hold values from -0.0625 to 0.0625
- channel_scale: float32 [8192], P('tensor')
- lengths: int32 [16], P('dp'), may hold values from 16 to 64, as said below
Outputs:
- direction: float32 [8192, 8192], P('dp', 'tensor')
- loss: float32 [], replicated
Inputs may be any that keep to these rules, and one draw needn't show every extreme that they name: `lengths`: each sequence's valid length; some sequence is full in every draw.
All inputs are finite; a program needn't handle non-finite values.
Results may differ from a plain program's by a relative error of at most 0.00075.
The roundings to bfloat16 on the way count: a program that leaves them out, or rounds other values in their place, can miss the bound.
Values may be sent and summed in bfloat16 or wider, within the bound.
A program may use at most 128 MiB of HBM per device.

v0:
```python
import math
import jax
import jax.numpy as jnp
from jax import lax
from jax.sharding import PartitionSpec as P

D = 8192
SEQ = 64


def local(hidden, rotation, channel_scale, lengths):
    narrow_rotation = rotation.astype(jnp.bfloat16)
    features = lax.all_gather(hidden, "tensor", axis=1, tiled=True)
    column_blocks = lax.all_to_all(features, "dp", split_axis=1, concat_axis=0, tiled=True)
    partial = jnp.dot(column_blocks, narrow_rotation, preferred_element_type=jnp.float32)
    rotated = lax.psum_scatter(partial, "dp", scatter_dimension=0, tiled=True)
    scaled = rotated * channel_scale[None, :]
    token_square = lax.psum(jnp.sum(scaled * scaled, axis=1), "tensor")
    step_size = 4.0 * jnp.sqrt(token_square / D + 1e-06)[:, None]
    token_index = jnp.arange(hidden.shape[0], dtype=jnp.int32)
    position = token_index % SEQ
    sequence_index = token_index // SEQ
    sequence_count = lengths.shape[0]
    owners = sequence_index[:, None] == jnp.arange(sequence_count, dtype=jnp.int32)[None, :]
    inside = position[:, None] < lengths[None, :]
    live_mask = jnp.sum(jnp.where(owners & inside, 1.0, 0.0), axis=1).astype(jnp.float32)[:, None]
    angles = math.pi * scaled / step_size
    error_local = jnp.sum(live_mask * jnp.sin(angles) ** 2)
    count_local = jnp.sum(lengths).astype(jnp.float32) / lax.axis_size("tensor")
    error_slope = (
        live_mask * (math.pi / step_size) * jnp.sin(2.0 * angles) * channel_scale[None, :]
    ).astype(jnp.bfloat16)
    gradient = lax.dot_general(
        column_blocks,
        lax.all_gather(error_slope, "dp", axis=0, tiled=True),
        (((0,), (0,)), ((), ())),
        preferred_element_type=jnp.float32,
    )
    error_sum, count = lax.psum((error_local, count_local), ("dp", "tensor"))
    grad_square = lax.psum(jnp.sum(gradient * gradient), ("dp", "tensor"))
    direction = gradient / jnp.sqrt(grad_square / (D * D) + 1e-06)
    loss = error_sum / (D * count)
    return (direction, loss)


def solution(mesh):
    return jax.shard_map(
        local,
        mesh=mesh,
        in_specs=(P("dp", "tensor"), P("dp", "tensor"), P("tensor"), P("dp")),
        out_specs=(P("dp", "tensor"), P()),
        check_vma=False,
    )
```

profile of v0, /device:TPU:0, one launch (start us, length us, event | category | flops | bytes accessed | tf_op | source)
XLA Modules:
  0.0 305.9 jit_solution(8076852472374651479)
XLA Ops:
  7.2 0.0 all-gather.3.cloned.1.call-start
  7.2 2.0 copy.11
  9.3 0.0 all-gather.3.cloned.1.call-update
  9.3 0.0 reduce-scatter.2.cloned.1.call-start
  9.3 49.5 %all-gather.3.cloned.1.call-done = bf16[128,8192]{0,1:T(8,128)(2,1)} async-done(((bf16[128,2048]{0,1:T(8,128)(2,1)}), bf16[128,8192]{0,1:T(8,128)(2,1)}) %all-gather.3.cloned.1.call-update) | async-done | bytes 2097168 | tf_op jit(solution)/shard_map/all_gather | solution.py:13
  58.8 30.2 %all_to_all.19 = bf16[128,8,1024]{0,2,1:T(8,128)(2,1)S(1)} all-to-all(bf16[128,8,1024]{0,2,1:T(8,128)(2,1)} %bitcast.11), channel_id=1, replica_groups=mesh['dp'=8,'tensor'=4] {'dp'}, dimensions={1} | all-to-all | bytes 4194304 | tf_op jit(solution)/shard_map/all_to_all | solution.py:14
  89.0 2.6 copy.12
  91.6 11.9 %fusion = f32[1024,2048]{1,0:T(8,128)} fusion(bf16[1024,1024]{1,0:T(8,128)(2,1)} %bitcast.9, f32[1024,2048]{1,0:T(8,128)} %param.5), kind=kOutput, calls=%fused_computation.2 | convolution fusion | flops 4297064448 | bytes 18874368 | tf_op jit(solution)/shard_map/dot_general | solution.py:15
  103.6 0.0 copy-start.2
  103.6 0.0 copy-start.1
  103.6 0.0 copy-start
  103.6 0.0 reduce-scatter.2.cloned.1.call-update
  103.6 0.0 all-gather.5.cloned.1.call-start
  103.6 0.6 copy-done.2
  104.2 0.1 fusion.2
  104.3 67.6 %reduce-scatter.2.cloned.1.call-done = f32[128,2048]{1,0:T(8,128)} async-done(((f32[1024,2048]{1,0:T(8,128)}), f32[128,2048]{1,0:T(8,128)}) %reduce-scatter.2.cloned.1.call-update) | async-done | bytes 1048592 | tf_op jit(solution)/shard_map/reduce_scatter | solution.py:16
  171.9 0.0 copy-done.1
  171.9 1.4 multiply_reduce_fusion.2
  173.3 11.7 %psum.28 = f32[128]{0:T(128)S(1)} all-reduce(f32[128]{0:T(128)S(1)} %multiply_reduce_fusion.2), channel_id=1, replica_groups=mesh['dp'=8,'tensor'=4] {'tensor'}, use_global_device_ids=true, to_apply=%region_3.4 | all-reduce | flops 128 | bytes 1024 | tf_op jit(solution)/shard_map/psum | solution.py:18
  185.0 9.9 %multiply_reduce_fusion.1 = (f32[]{:T(128)}, bf16[128,2048]{1,0:T(8,128)(2,1)}) fusion(f32[128]{0:T(128)S(1)} %fusion.2, f32[128]{0:T(128)S(1)} %get-tuple-element.15, f32[128,2048]{1,0:T(8,128)} %reduce-scatter.2.cloned.1.call-done, f32[2048]{0:T(1024)S(1)} %copy-done.1, f32[128]{0:T(128)S(1)} %get-tuple-element.16), kind=kLoop, calls=%fused_computation.4 | loop fusion | flops 2621439 | bytes 1582596 | tf_op jit(solution)/shard_map/reduce_sum | solution.py:28
  194.9 0.0 all-gather.5.cloned.1.call-update
  195.0 0.6 reduce_sum.49
  196.2 32.9 %all-gather.5.cloned.1.call-done = bf16[1024,2048]{1,0:T(8,128)(2,1)} async-done(((bf16[128,2048]{1,0:T(8,128)(2,1)}), bf16[1024,2048]{1,0:T(8,128)(2,1)}) %all-gather.5.cloned.1.call-update) | async-done | bytes 4194320 | tf_op jit(solution)/shard_map/all_gather | solution.py:35
  229.0 0.0 copy-done
  229.1 10.1 %multiply_reduce_fusion = (f32[]{:T(128)}, f32[2048,1024]{1,0:T(8,128)}) fusion(bf16[1024,2048]{1,0:T(8,128)(2,1)} %all-gather.5.cloned.1.call-done, bf16[1024,1024]{1,0:T(8,128)(2,1)S(1)} %bitcast.10), kind=kOutput, calls=%fused_computation.1 | convolution fusion | flops 4299161600 | bytes 14680068 | tf_op jit(solution)/shard_map/dot_general | solution.py:33
  239.2 39.6 %all-reduce = (f32[]{:T(128)}, f32[]{:T(128)}, f32[]{:T(128)}) all-reduce(f32[]{:T(128)} %get-tuple-element.17, f32[]{:T(128)} %get-tuple-element.13, f32[]{:T(128)S(6)} %div.59), channel_id=1, replica_groups=mesh['dp'=8,'tensor'=4] {'dp','tensor'}, use_global_device_ids=true, to_apply=%region_5.6 | all-reduce | flops 3 | bytes 24 | tf_op jit(solution)/shard_map/psum | solution.py:40
  279.4 8.5 %divide_bitcast_fusion = f32[1024,2048]{0,1:T(8,128)} fusion(f32[2048,1024]{1,0:T(8,128)} %get-tuple-element.18, f32[]{:T(128)S(6)} %sqrt.7), kind=kLoop, calls=%fused_computation | loop fusion | flops 2097152 | bytes 16777220 | tf_op jit(solution)/shard_map/div | solution.py:41
  287.9 9.1 %copy.13 = f32[1024,2048]{1,0:T(8,128)} copy(f32[1024,2048]{0,1:T(8,128)} %divide_bitcast_fusion) | data formatting | bytes 16777216
  (2 shorter events, 0.0 us)
Async XLA Ops:
  7.2 51.6 %all-gather.3.cloned.1.call-start = ((), (), s32[]{:S(2)}) async-start(), calls=%async_computation.2 | async-start | bytes 2621440 | tf_op jit(solution)/shard_map/all_gather | solution.py:13
  9.3 162.6 %reduce-scatter.2.cloned.1.call-start = ((), (), s32[]{:S(2)}) async-start(), calls=%async_computation.3 | async-start | bytes 9437184 | tf_op jit(solution)/shard_map/reduce_scatter | solution.py:16
  103.6 0.7 copy-start.2
  103.6 68.4 %copy-start.1 = (f32[2048]{0:T(1024)S(1)}, f32[2048]{0:T(1024)}, u32[]{:S(2)}) copy-start(f32[2048]{0:T(1024)} %param.6) | copy-start | bytes 24580
  103.6 125.5 %copy-start = (bf16[8,128,1024]{2,1,0:T(8,128)(2,1)S(1)}, bf16[8,128,1024]{2,1,0:T(8,128)(2,1)}, u32[]{:S(2)}) copy-start(bf16[8,128,1024]{2,1,0:T(8,128)(2,1)} %copy.12) | copy-start | bytes 6291460
  103.6 125.5 %all-gather.5.cloned.1.call-start = ((), (), s32[]{:S(2)}) async-start(), calls=%async_computation.4 | async-start | bytes 4718592 | tf_op jit(solution)/shard_map/all_gather | solution.py:35
Sparse Core Ops, SparseCore 0:
  10.1 48.6 all-gather.2
  103.7 68.1 reduce-scatter.1
  195.1 33.9 all-gather.4
where the time goes:
time: 307 us; the launch traced here: 306 us
  waiting for transfers between devices  150 us (49%)
  blocking collectives  81.5 us (27%)
  matrix products  22 us (7%)
  other arithmetic  20.6 us (7%)
  between operations  17.3 us (6%)
  local copies, waits for them, and re-layouts  14.3 us (5%)
    reduce_scatter x1, waiting for transfers between devices, local(): rotated = lax.psum_scatter(partial, 'dp', scatter_dimension=0, tiled=True)  67.6 us
    all_gather x1, waiting for transfers between devices, local(): features = lax.all_gather(hidden, 'tensor', axis=1, tiled=True)  49.5 us
    psum x1, blocking collectives, local(): grad_square = lax.psum(jnp.sum(gradient * gradient), ('dp', 'tensor'))  39.6 us
    all_gather x1, waiting for transfers between devices, local(): lax.all_gather(error_slope, 'dp', axis=0, tiled=True)  32.9 us
    all_to_all x1, blocking collectives, local(): lax.all_to_all(features, 'dp', split_axis=1, concat_axis=0, tiled=True)  30.2 us
    dot_general x1, matrix products, local(): jnp.dot(column_blocks, narrow_rotation, preferred_element_type=jnp.float32)  11.9 us
    unnamed x8, local copies, waits for them, and re-layouts  11.7 us
    psum x1, blocking collectives, local(): token_square = lax.psum(jnp.sum(scaled * scaled, axis=1), 'tensor')  11.7 us
  transfers between devices with their start and end apart: 3, of which 3 were waited for; matrix products, arithmetic and copies ran while one was open for 0% of the time, Pallas kernels for 0%

commit v1 on v0

--- a/solution.py
+++ b/solution.py
@@ -10,7 +10,14 @@
 
 def local(hidden, rotation, channel_scale, lengths):
     narrow_rotation = rotation.astype(jnp.bfloat16)
-    features = lax.all_gather(hidden, "tensor", axis=1, tiled=True)
+    ring = [hidden]
+    for hop in range(3):
+        ring.append(lax.ppermute(ring[-1], "tensor", [(dev, (dev + 1) % 4) for dev in range(4)]))
+    features = jnp.roll(
+        jnp.concatenate(ring[::-1], axis=1),
+        (lax.axis_index("tensor") + 1) * ring[0].shape[1],
+        axis=1,
+    )
     column_blocks = lax.all_to_all(features, "dp", split_axis=1, concat_axis=0, tiled=True)
     partial = jnp.dot(column_blocks, narrow_rotation, preferred_element_type=jnp.float32)
     rotated = lax.psum_scatter(partial, "dp", scatter_dimension=0, tiled=True)

time: 307 us -> 293 us (0.954)
  local copies, waits for them, and re-layouts: 14.3 us -> 5.15 us
  waiting for transfers between devices: 150 us -> 143 us
    all_gather x1 -> x0, waiting for transfers between devices: 49.5 us -> none  [local(): features = lax.all_gather(hidden, 'tensor', axis=1, tiled=True)]
    ppermute x0 -> x3, waiting for transfers between devices: none -> 42.8 us  [local(): lax.ppermute(ring[-1], 'tensor', [(dev, (dev + 1) % 4) for dev in range(4)])]
    unnamed x8 -> x14, local copies, waits for them, and re-layouts: 11.7 us -> 2.34 us
    ppermute x0 -> x3, starting transfers between devices: none -> 3.08 us  [local(): lax.ppermute(ring[-1], 'tensor', [(dev, (dev + 1) % 4) for dev in range(4)])]
  transfers between devices with their start and end apart: 3 -> 5, of which waited for: 3 -> 5; matrix products, arithmetic and copies ran while one was open for 0% -> 0% of each run, Pallas kernels for 0% -> 0%
where the time goes in v1:
time: 293 us; the launch traced here: 292 us
  waiting for transfers between devices  143 us (49%)
  blocking collectives  80.9 us (28%)
  matrix products  22.1 us (8%)
  other arithmetic  20.5 us (7%)
  between operations  17.8 us (6%)
  local copies, waits for them, and re-layouts  5.15 us (2%)
  starting transfers between devices  3.16 us (1%)
    reduce_scatter x1, waiting for transfers between devices, local(): rotated = lax.psum_scatter(partial, 'dp', scatter_dimension=0, tiled=True)  67.1 us
    ppermute x3, waiting for transfers between devices, local(): lax.ppermute(ring[-1], 'tensor', [(dev, (dev + 1) % 4) for dev in range(4)])  42.8 us
    psum x1, blocking collectives, local(): grad_square = lax.psum(jnp.sum(gradient * gradient), ('dp', 'tensor'))  39.6 us
    all_gather x1, waiting for transfers between devices, local(): lax.all_gather(error_slope, 'dp', axis=0, tiled=True)  32.9 us
    all_to_all x1, blocking collectives, local(): lax.all_to_all(features, 'dp', split_axis=1, concat_axis=0, tiled=True)  29.6 us
    dot_general x1, matrix products, local(): jnp.dot(column_blocks, narrow_rotation, preferred_element_type=jnp.float32)  11.9 us
    psum x1, blocking collectives, local(): token_square = lax.psum(jnp.sum(scaled * scaled, axis=1), 'tensor')  11.7 us
    dot_general x1, matrix products, local(): lax.dot_general(column_blocks, lax.all_gather(error_slope, 'dp', axis=0,...  10.2 us
  transfers between devices with their start and end apart: 5, of which 5 were waited for; matrix products, arithmetic and copies ran while one was open for 0% of the time, Pallas kernels for 0%

profile of v1, /device:TPU:0, one launch (start us, length us, event | category | flops | bytes accessed | tf_op | source)
XLA Modules:
  0.0 292.4 jit_solution(8945472084123297363)
XLA Ops:
  7.2 0.0 reduce-scatter.2.cloned.1.call-start
  7.2 1.3 copy.10
  8.5 3.1 %collective-permute-start = (bf16[128,2048]{0,1:T(8,128)(2,1)S(1)}, bf16[128,2048]{0,1:T(8,128)(2,1)S(1)}, u32[]{:S(2)}, u32[]{:S(2)}) collective-permute-start(bf16[128,2048]{0,1:T(8,128)(2,1)S(1)} %copy.10), channel_id=1, source_target_pairs={{0,1},{1,2},{2,3},{3,0},{4,5},{5,6},{6,7},{7,4},{8,9},{9,10},{10,1... | collective-permute-start | bytes 1572872 | tf_op jit(solution)/shard_map/ppermute | solution.py:15
  11.6 13.9 %collective-permute-done = bf16[128,2048]{0,1:T(8,128)(2,1)S(1)} collective-permute-done((bf16[128,2048]{0,1:T(8,128)(2,1)S(1)}, bf16[128,2048]{0,1:T(8,128)(2,1)S(1)}, u32[]{:S(2)}, u32[]{:S(2)}) %collective-permute-start) | collective-permute-done | bytes 524320 | tf_op jit(solution)/shard_map/ppermute | solution.py:15
  25.6 0.0 collective-permute-start.1
  25.6 14.9 %collective-permute-done.1 = bf16[128,2048]{0,1:T(8,128)(2,1)S(1)} collective-permute-done((bf16[128,2048]{0,1:T(8,128)(2,1)S(1)}, bf16[128,2048]{0,1:T(8,128)(2,1)S(1)}, u32[]{:S(2)}, u32[]{:S(2)}) %collective-permute-start.1) | collective-permute-done | bytes 524320 | tf_op jit(solution)/shard_map/ppermute | solution.py:15
  40.5 0.0 collective-permute-start.2
  40.5 14.0 %collective-permute-done.2 = bf16[128,2048]{0,1:T(8,128)(2,1)S(1)} collective-permute-done((bf16[128,2048]{0,1:T(8,128)(2,1)S(1)}, bf16[128,2048]{0,1:T(8,128)(2,1)S(1)}, u32[]{:S(2)}, u32[]{:S(2)}) %collective-permute-start.2) | collective-permute-done | bytes 524320 | tf_op jit(solution)/shard_map/ppermute | solution.py:15
  54.5 0.1 constant_dynamic-update-slice_fusion.6
  54.6 0.1 constant_dynamic-update-slice_fusion.5
  54.6 0.1 constant_dynamic-update-slice_fusion.4
  54.7 0.1 constant_dynamic-update-slice_fusion.3
  54.8 0.1 constant_dynamic-update-slice_fusion.2
  54.9 0.1 constant_dynamic-update-slice_fusion.1
  55.0 0.1 constant_dynamic-update-slice_fusion
  55.0 0.1 constant_dynamic-slice_fusion
  55.2 29.6 %all_to_all.19 = bf16[128,8,1024]{0,2,1:T(8,128)(2,1)S(1)} all-to-all(bf16[128,8,1024]{0,2,1:T(8,128)(2,1)S(1)} %bitcast.6), channel_id=1, replica_groups=mesh['dp'=8,'tensor'=4] {'dp'}, dimensions={1} | all-to-all | bytes 4194304 | tf_op jit(solution)/shard_map/all_to_all | solution.py:21
  84.8 2.6 copy.13
  87.4 11.9 %fusion = f32[1024,2048]{1,0:T(8,128)} fusion(bf16[1024,1024]{1,0:T(8,128)(2,1)} %bitcast.8, f32[1024,2048]{1,0:T(8,128)} %param.5), kind=kOutput, calls=%fused_computation.2 | convolution fusion | flops 4297064448 | bytes 18874368 | tf_op jit(solution)/shard_map/dot_general | solution.py:22
  99.3 0.0 copy-start.2
  99.3 0.0 copy-start.1
  99.3 0.0 copy-start
  99.3 0.0 reduce-scatter.2.cloned.1.call-update
  99.4 0.0 all-gather.2.cloned.1.call-start
  99.4 0.6 copy-done.2
  100.0 0.1 fusion.2
  100.1 67.1 %reduce-scatter.2.cloned.1.call-done = f32[128,2048]{1,0:T(8,128)} async-done(((f32[1024,2048]{1,0:T(8,128)}), f32[128,2048]{1,0:T(8,128)}) %reduce-scatter.2.cloned.1.call-update) | async-done | bytes 1048592 | tf_op jit(solution)/shard_map/reduce_scatter | solution.py:23
  167.1 0.0 copy-done.1
  167.1 1.4 multiply_reduce_fusion.2
  168.5 11.7 %psum.28 = f32[128]{0:T(128)S(1)} all-reduce(f32[128]{0:T(128)S(1)} %multiply_reduce_fusion.2), channel_id=1, replica_groups=mesh['dp'=8,'tensor'=4] {'tensor'}, use_global_device_ids=true, to_apply=%region_3.4 | all-reduce | flops 128 | bytes 1024 | tf_op jit(solution)/shard_map/psum | solution.py:25
  180.2 9.9 %multiply_reduce_fusion.1 = (f32[]{:T(128)}, bf16[128,2048]{1,0:T(8,128)(2,1)}) fusion(f32[128]{0:T(128)S(1)} %fusion.2, f32[128]{0:T(128)S(1)} %get-tuple-element.7, f32[128,2048]{1,0:T(8,128)} %reduce-scatter.2.cloned.1.call-done, f32[2048]{0:T(1024)S(1)} %copy-done.1, f32[128]{0:T(128)S(1)} %get-tuple-element.8), kind=kLoop, calls=%fused_computation.4 | loop fusion | flops 2621439 | bytes 1582596 | tf_op jit(solution)/shard_map/reduce_sum | solution.py:35
  190.1 0.0 all-gather.2.cloned.1.call-update
  190.2 0.6 reduce_sum.49
  191.4 32.9 %all-gather.2.cloned.1.call-done = bf16[1024,2048]{1,0:T(8,128)(2,1)} async-done(((bf16[128,2048]{1,0:T(8,128)(2,1)}), bf16[1024,2048]{1,0:T(8,128)(2,1)}) %all-gather.2.cloned.1.call-update) | async-done | bytes 4194320 | tf_op jit(solution)/shard_map/all_gather | solution.py:42
  224.3 0.0 copy-done
  224.3 10.2 %multiply_reduce_fusion = (f32[]{:T(128)}, f32[1024,2048]{1,0:T(8,128)}) fusion(bf16[1024,1024]{1,0:T(8,128)(2,1)S(1)} %bitcast.9, bf16[1024,2048]{1,0:T(8,128)(2,1)} %all-gather.2.cloned.1.call-done), kind=kOutput, calls=%fused_computation | convolution fusion | flops 4299161600 | bytes 14680068 | tf_op jit(solution)/shard_map/dot_general | solution.py:40
  234.5 39.6 %all-reduce = (f32[]{:T(128)}, f32[]{:T(128)}, f32[]{:T(128)}) all-reduce(f32[]{:T(128)} %get-tuple-element.9, f32[]{:T(128)} %get-tuple-element.5, f32[]{:T(128)S(6)} %div.55), channel_id=1, replica_groups=mesh['dp'=8,'tensor'=4] {'dp','tensor'}, use_global_device_ids=true, to_apply=%region_5.6 | all-reduce | flops 3 | bytes 24 | tf_op jit(solution)/shard_map/psum | solution.py:47
  276.0 8.4 %broadcast_divide_fusion = f32[1024,2048]{1,0:T(8,128)} fusion(f32[1024,2048]{1,0:T(8,128)} %get-tuple-element.10, f32[]{:T(128)S(6)} %sqrt.7), kind=kLoop, calls=%fused_computation.1 | loop fusion | flops 2097152 | bytes 16777220 | tf_op jit(solution)/shard_map/div | solution.py:48
  (3 shorter events, 0.1 us)
Async XLA Ops:
  7.2 160.0 %reduce-scatter.2.cloned.1.call-start = ((), (), s32[]{:S(2)}) async-start(), calls=%async_computation.2 | async-start | bytes 9437184 | tf_op jit(solution)/shard_map/reduce_scatter | solution.py:23
  8.5 17.0 %collective-permute-start = (bf16[128,2048]{0,1:T(8,128)(2,1)S(1)}, bf16[128,2048]{0,1:T(8,128)(2,1)S(1)}, u32[]{:S(2)}, u32[]{:S(2)}) collective-permute-start(bf16[128,2048]{0,1:T(8,128)(2,1)S(1)} %copy.10), channel_id=1, source_target_pairs={{0,1},{1,2},{2,3},{3,0},{4,5},{5,6},{6,7},{7,4},{8,9},{9,10},{10,1... | collective-permute-start | bytes 1572872 | tf_op jit(solution)/shard_map/ppermute | solution.py:15
  25.6 14.9 %collective-permute-start.1 = (bf16[128,2048]{0,1:T(8,128)(2,1)S(1)}, bf16[128,2048]{0,1:T(8,128)(2,1)S(1)}, u32[]{:S(2)}, u32[]{:S(2)}) collective-permute-start(bf16[128,2048]{0,1:T(8,128)(2,1)S(1)} %collective-permute-done), channel_id=1, source_target_pairs={{0,1},{1,2},{2,3},{3,0},{4,5},{5,6},{6,7},{7,4},{8,9},{9,10},{10,1... | collective-permute-start | bytes 1572872 | tf_op jit(solution)/shard_map/ppermute | solution.py:15
  40.5 14.0 %collective-permute-start.2 = (bf16[128,2048]{0,1:T(8,128)(2,1)S(1)}, bf16[128,2048]{0,1:T(8,128)(2,1)S(1)}, u32[]{:S(2)}, u32[]{:S(2)}) collective-permute-start(bf16[128,2048]{0,1:T(8,128)(2,1)S(1)} %collective-permute-done.1), channel_id=1, source_target_pairs={{0,1},{1,2},{2,3},{3,0},{4,5},{5,6},{6,7},{7,4},{8,9},{9,10},{10,1... | collective-permute-start | bytes 1572872 | tf_op jit(solution)/shard_map/ppermute | solution.py:15
  99.3 0.7 copy-start.2
  99.3 67.8 %copy-start.1 = (f32[2048]{0:T(1024)S(1)}, f32[2048]{0:T(1024)}, u32[]{:S(2)}) copy-start(f32[2048]{0:T(1024)} %param.6) | copy-start | bytes 24580
  99.3 124.9 %copy-start = (bf16[8,128,1024]{2,1,0:T(8,128)(2,1)S(1)}, bf16[8,128,1024]{2,1,0:T(8,128)(2,1)}, u32[]{:S(2)}) copy-start(bf16[8,128,1024]{2,1,0:T(8,128)(2,1)} %copy.13) | copy-start | bytes 6291460
  99.4 124.9 %all-gather.2.cloned.1.call-start = ((), (), s32[]{:S(2)}) async-start(), calls=%async_computation.3 | async-start | bytes 4718592 | tf_op jit(solution)/shard_map/all_gather | solution.py:42
Sparse Core Ops, SparseCore 0:
  99.5 67.6 reduce-scatter.1
  190.3 33.9 all-gather.1
